TPU v7x, 32 devices: a whole 2x2x4 slice. The times are simulated.
32 devices in a mesh: dp: 2 (over x), expert: 16 (over z, y, core).
Axes of the slice: x: 2, y: 2, z: 4, core: 2. Of those that a mesh axis runs over, the one named last changes fastest.
Arguments:
- tokens: bfloat16 [4096, 512], P(('dp', 'expert')), may hold values from -6 to 6
- modality: int32 [4096], P(('dp', 'expert')), may hold values 0 or 1
- modal_gains: float32 [2, 512], replicated, may hold values from 0.5 to 2
- routes: int32 [4096, 2], P(('dp', 'expert')), may hold values from 0 to 15, all different within a row; in each aligned block of 128 rows (0 to 127, 128 to 255, ...) at most 32 rows name the same one
- gate_share: int32 [4096], P(('dp', 'expert')), may hold values from 1 to 15
- up_weight: bfloat16 [16, 2048, 512], P('expert', 'dp'), may hold values from -0.25 to 0.25
- down_weight: bfloat16 [16, 2048, 512], P('expert', 'dp'), may hold values from -0.125 to 0.125
- cotangent: bfloat16 [4096, 512], P(('dp', 'expert')), may hold values from -6 to 6
Outputs:
- moe_output: bfloat16 [4096, 512], P(('dp', 'expert'))
- token_grad: bfloat16 [4096, 512], P(('dp', 'expert'))
- up_grad: bfloat16 [16, 2048, 512], P('expert', 'dp')
- down_grad: bfloat16 [16, 2048, 512], P('expert', 'dp')
Inputs may be any that keep to these rules, and one draw needn't show every extreme that they name: `routes`: each row names two different experts; among the 128 rows of one device no expert is named more than 32 times, and in every draw some device names some expert exactly 32 times.
All inputs are finite; a program needn't handle non-finite values. No bound on the sum of `modality` on one device may be relied on, other than what follows from the above.
Results may differ from a plain program's by a relative error of at most 0.014.
Values may be sent and summed in bfloat16 or wider, within the bound.
A program may use at most 64 MiB of HBM per device.

v0:
```python
import math

import jax
import jax.numpy as jnp
from jax import lax
from jax.sharding import PartitionSpec as P

root_half = 0.7071067811865476
density = 0.3989422804014327


def gelu_value(values):
    return values * 0.5 * (1.0 + lax.erf(values * root_half))


def gelu_slope(values):
    return (
        0.5 * (1.0 + lax.erf(values * root_half))
        + values * jnp.exp(-0.5 * values * values) * density
    )


def row_product(left_side, right_side, right_axis):
    numbers = (((1,), (right_axis,)), ((), ()))
    return lax.dot_general(left_side, right_side, numbers, preferred_element_type=jnp.float32)


def row_contract(left_side, right_side):
    numbers = (((0,), (0,)), ((), ()))
    return lax.dot_general(left_side, right_side, numbers, preferred_element_type=jnp.float32)


def on_device(tokens, modality, modal_gains, routes, gate_share, up_weight, down_weight, cotangent):
    tok_count = tokens.shape[0]
    model_width = tokens.shape[1]
    expert_count = lax.axis_size("expert")
    replica_count = lax.axis_size("dp")
    capacity = 4 * tok_count // expert_count
    slot_count = expert_count * capacity
    grad_scale = 1.0 / math.sqrt(2 * tok_count * replica_count)
    x_float = tokens.astype(jnp.float32)
    inv_rms = lax.rsqrt(jnp.mean(x_float * x_float, axis=-1, keepdims=True) + 1e-06)
    gain_rows = jnp.where(modality[:, None] == 1, modal_gains[1][None, :], modal_gains[0][None, :])
    normed = (x_float * inv_rms * gain_rows).astype(jnp.bfloat16)
    gate_first = gate_share.astype(jnp.float32) / 16.0
    gate_pair = jnp.stack([gate_first, 1.0 - gate_first], axis=1)
    flat_routes = routes.reshape(-1)
    one_hot = (flat_routes[:, None] == jnp.arange(expert_count, dtype=jnp.int32)[None, :]).astype(
        jnp.int32
    )
    earlier = jnp.cumsum(one_hot, axis=0) - one_hot
    position = jnp.sum(earlier * one_hot, axis=1)
    slot_index = flat_routes * capacity + position
    normed_routes = jnp.repeat(normed, 2, axis=0)
    empty_rows = jnp.zeros((slot_count, model_width), jnp.bfloat16)
    send_rows = (
        empty_rows.at[slot_index].set(normed_routes).reshape(expert_count, capacity, model_width)
    )
    route_grad = (
        (gate_pair[:, :, None] * cotangent.astype(jnp.float32)[:, None, :])
        .astype(jnp.bfloat16)
        .reshape(2 * tok_count, model_width)
    )
    send_grad = (
        empty_rows.at[slot_index].set(route_grad).reshape(expert_count, capacity, model_width)
    )
    sent_counts = jnp.sum(one_hot, axis=0).astype(jnp.bfloat16).reshape(expert_count, 1)
    arrived, arrived_counts = (
        lax.all_to_all(send_rows, "expert", split_axis=0, concat_axis=0, tiled=True),
        lax.all_to_all(sent_counts, "expert", split_axis=0, concat_axis=0, tiled=True),
    )
    expert_rows = arrived.reshape(slot_count, model_width)
    pre_act = row_product(expert_rows, lax.all_gather(up_weight, "dp", axis=1, tiled=True)[0], 1)
    activated = gelu_value(pre_act).astype(jnp.bfloat16)
    act_part = activated
    expert_out = row_product(act_part, lax.all_gather(down_weight, "dp", axis=1, tiled=True)[0], 0)
    outgoing = expert_out.astype(jnp.bfloat16).reshape(expert_count, capacity, model_width)
    back_rows = lax.all_to_all(outgoing, "expert", split_axis=0, concat_axis=0, tiled=True)
    arrived_grad = lax.all_to_all(send_grad, "expert", split_axis=0, concat_axis=0, tiled=True)
    grad_rows = arrived_grad.reshape(slot_count, model_width)
    hidden_grad = row_product(
        grad_rows, lax.all_gather(down_weight, "dp", axis=1, tiled=True)[0], 1
    )
    pre_grad = (hidden_grad * gelu_slope(pre_act)).astype(jnp.bfloat16)
    grad_part = pre_grad
    normed_part = row_product(grad_part, lax.all_gather(up_weight, "dp", axis=1, tiled=True)[0], 0)
    returning = normed_part.astype(jnp.bfloat16).reshape(expert_count, capacity, model_width)
    back_grad = lax.all_to_all(returning, "expert", split_axis=0, concat_axis=0, tiled=True)
    route_out = (
        back_rows.reshape(slot_count, model_width)[slot_index]
        .astype(jnp.float32)
        .reshape(tok_count, 2, model_width)
    )
    moe_output = jnp.sum(gate_pair[:, :, None] * route_out, axis=1).astype(jnp.bfloat16)
    route_back = (
        back_grad.reshape(slot_count, model_width)[slot_index]
        .astype(jnp.float32)
        .reshape(tok_count, 2, model_width)
    )
    normed_grad = jnp.sum(route_back, axis=1)
    scaled = gain_rows * normed_grad
    token_grad = (
        inv_rms * scaled - x_float * inv_rms**3 * jnp.mean(x_float * scaled, axis=-1, keepdims=True)
    ).astype(jnp.bfloat16)
    grad_part = pre_grad
    act_part = activated
    up_term = row_contract(grad_part, expert_rows)
    down_term = row_contract(act_part, grad_rows)
    grad_pair = lax.psum_scatter(
        (jnp.stack([up_term, down_term], axis=1) * grad_scale).astype(jnp.bfloat16),
        "dp",
        scatter_dimension=0,
        tiled=True,
    ).astype(jnp.float32)
    up_grad = grad_pair[:, 0][None].astype(jnp.bfloat16)
    down_grad = grad_pair[:, 1][None].astype(jnp.bfloat16)
    return (moe_output, token_grad, up_grad, down_grad)


def solution(mesh):
    placed = (
        P(("dp", "expert"), None),
        P(("dp", "expert")),
        P(),
        P(("dp", "expert"), None),
        P(("dp", "expert")),
        P("expert", "dp", None),
        P("expert", "dp", None),
        P(("dp", "expert"), None),
    )
    return jax.shard_map(
        on_device,
        mesh=mesh,
        in_specs=placed,
        out_specs=(
            P(("dp", "expert"), None),
            P(("dp", "expert"), None),
            P("expert", "dp", None),
            P("expert", "dp", None),
        ),
        check_vma=False,
    )
```

profile of v0, /device:TPU:0, one launch (start us, length us, event | category | flops | bytes accessed | tf_op | source)
XLA Modules:
  0.0 153.7 jit_solution(14276396266286236889)
XLA Ops:
  15.3 2.3 %scatter_custom_fusion = bf16[512,512]{1,0:T(8,128)(2,1)} fusion(s32[256]{0:T(256)S(1)} %bitcast.81, bf16[256,512]{1,0:T(8,128)(2,1)S(1)} %reshape.172, bf16[]{:T(256)} %constant.17.clone.1), kind=kCustom, calls=%fused_computation.45 | custom fusion | bytes 524290 | tf_op jit(solution)/shard_map/scatter | solution.py:57
  17.7 7.4 %all-to-all-start = ((bf16[16,32,512]{2,1,0:T(8,128)(2,1)}), bf16[16,32,512]{2,1,0:T(8,128)(2,1)S(1)}, u32[]{:S(2)}, u32[]{:S(2)}) async-start(bf16[16,32,512]{2,1,0:T(8,128)(2,1)} %bitcast.7), calls=%async_computation | async-start | bytes 1048576 | tf_op jit(solution)/shard_map/all_to_all | solution.py:69
  25.9 2.4 %scatter_custom_fusion.1 = bf16[512,512]{1,0:T(8,128)(2,1)} fusion(s32[256]{0:T(256)S(1)} %bitcast.82, f32[256,512]{1,0:T(8,128)S(1)} %mul.143, f32[256]{0:T(256)S(1)} %mul.140, bf16[]{:T(256)} %constant.17.clone.1), kind=kCustom, calls=%fused_computation.42 | custom fusion | flops 262144 | bytes 1049602 | tf_op jit(solution)/shard_map/scatter | solution.py:65
  28.2 11.3 %all-to-all-done = bf16[16,32,512]{2,1,0:T(8,128)(2,1)S(1)} async-done(((bf16[16,32,512]{2,1,0:T(8,128)(2,1)}), bf16[16,32,512]{2,1,0:T(8,128)(2,1)S(1)}, u32[]{:S(2)}, u32[]{:S(2)}) %all-to-all-start) | async-done | bytes 524320 | tf_op jit(solution)/shard_map/all_to_all | solution.py:69
  39.5 4.1 %all-to-all-start.2 = ((bf16[16,32,512]{2,1,0:T(8,128)(2,1)}), bf16[16,32,512]{2,1,0:T(8,128)(2,1)S(1)}, u32[]{:S(2)}, u32[]{:S(2)}) async-start(bf16[16,32,512]{2,1,0:T(8,128)(2,1)} %bitcast.13), calls=%async_computation.2 | async-start | bytes 1048576 | tf_op jit(solution)/shard_map/all_to_all | solution.py:79
  43.7 1.7 %all-gather.3.cloned.1.call-done = bf16[1,2048,512]{2,1,0:T(8,128)(2,1)} async-done(((bf16[1,1024,512]{2,1,0:T(8,128)(2,1)}), bf16[1,2048,512]{2,1,0:T(8,128)(2,1)}) %all-gather.3.cloned.1.call-update) | async-done | bytes 2097168 | tf_op jit(solution)/shard_map/all_gather | solution.py:73
  45.4 4.4 %multiply_convert_fusion = (bf16[512,2048]{1,0:T(8,128)(2,1)S(1)}, f32[512,2048]{1,0:T(8,128)}) fusion(bf16[512,512]{1,0:T(8,128)(2,1)S(1)} %bitcast.71, bf16[1,2048,512]{2,1,0:T(8,128)(2,1)} %all-gather.3.cloned.1.call-done), kind=kOutput, calls=%fused_computation.13 | convolution fusion | flops 1078984704 | bytes 8912896 | tf_op jit(solution)/shard_map/dot_general | solution.py:25
  49.8 8.2 %all-to-all-done.2 = bf16[16,32,512]{2,1,0:T(8,128)(2,1)S(1)} async-done(((bf16[16,32,512]{2,1,0:T(8,128)(2,1)}), bf16[16,32,512]{2,1,0:T(8,128)(2,1)S(1)}, u32[]{:S(2)}, u32[]{:S(2)}) %all-to-all-start.2) | async-done | bytes 524320 | tf_op jit(solution)/shard_map/all_to_all | solution.py:79
  58.1 22.0 %all-gather.5.cloned.1.call-done = bf16[1,2048,512]{2,1,0:T(8,128)(2,1)} async-done(((bf16[1,1024,512]{2,1,0:T(8,128)(2,1)}), bf16[1,2048,512]{2,1,0:T(8,128)(2,1)}) %all-gather.5.cloned.1.call-update) | async-done | bytes 2097168 | tf_op jit(solution)/shard_map/all_gather | solution.py:76
  80.1 4.4 %fusion.6 = bf16[512,2048]{1,0:T(8,128)(2,1)S(1)} fusion(f32[512,2048]{1,0:T(8,128)} %get-tuple-element.13, bf16[512,512]{1,0:T(8,128)(2,1)S(1)} %bitcast.73, bf16[1,2048,512]{2,1,0:T(8,128)(2,1)} %all-gather.5.cloned.1.call-done), kind=kOutput, calls=%fused_computation.12 | convolution fusion | flops 1084227584 | bytes 8912896 | tf_op jit(solution)/shard_map/dot_general | solution.py:25
  84.5 1.3 convolution_bitcast_fusion.1
  85.9 1.3 convolution_bitcast_fusion
  87.2 2.5 %fusion = bf16[2048,2,512]{2,0,1:T(8,128)(2,1)} fusion(f32[2048,1,512]{2,0,1:T(8,128)S(1)} %convolution_bitcast_fusion, f32[2048,1,512]{2,0,1:T(8,128)S(1)} %convolution_bitcast_fusion.1), kind=kLoop, calls=%fused_computation.5 | loop fusion | flops 6291456 | bytes 12582912 | tf_op jit(solution)/shard_map/convert_element_type | solution.py:110
  89.8 4.4 %fusion.17 = bf16[512,512]{1,0:T(8,128)(2,1)} fusion(bf16[512,2048]{1,0:T(8,128)(2,1)} %copy-done.4, bf16[1,2048,512]{2,1,0:T(8,128)(2,1)} %all-gather.5.cloned.1.call-done), kind=kOutput, calls=%fused_computation.25 | convolution fusion | flops 1074003968 | bytes 4718592 | tf_op jit(solution)/shard_map/dot_general | solution.py:25
  94.2 5.6 %all-to-all-start.1 = ((bf16[16,32,512]{2,1,0:T(8,128)(2,1)}), bf16[16,32,512]{2,1,0:T(8,128)(2,1)S(1)}, u32[]{:S(2)}, u32[]{:S(2)}) async-start(bf16[16,32,512]{2,1,0:T(8,128)(2,1)} %bitcast.11), calls=%async_computation.1 | async-start | bytes 1048576 | tf_op jit(solution)/shard_map/all_to_all | solution.py:78
  99.8 3.6 %fusion.14 = bf16[512,512]{1,0:T(8,128)(2,1)} fusion(bf16[512,2048]{1,0:T(8,128)(2,1)} %copy-done.5, bf16[1,2048,512]{2,1,0:T(8,128)(2,1)S(1)} %copy-done.2), kind=kOutput, calls=%fused_computation.24 | convolution fusion | flops 1074003968 | bytes 4718592 | tf_op jit(solution)/shard_map/dot_general | solution.py:25
  103.5 10.8 %all-to-all-done.1 = bf16[16,32,512]{2,1,0:T(8,128)(2,1)S(1)} async-done(((bf16[16,32,512]{2,1,0:T(8,128)(2,1)}), bf16[16,32,512]{2,1,0:T(8,128)(2,1)S(1)}, u32[]{:S(2)}, u32[]{:S(2)}) %all-to-all-start.1) | async-done | bytes 524320 | tf_op jit(solution)/shard_map/all_to_all | solution.py:78
  114.3 4.1 %all-to-all-start.3 = ((bf16[16,32,512]{2,1,0:T(8,128)(2,1)}), bf16[16,32,512]{2,1,0:T(8,128)(2,1)S(1)}, u32[]{:S(2)}, u32[]{:S(2)}) async-start(bf16[16,32,512]{2,1,0:T(8,128)(2,1)} %bitcast.15), calls=%async_computation.3 | async-start | bytes 1048576 | tf_op jit(solution)/shard_map/all_to_all | solution.py:88
  118.4 1.2 gather_fusion
  119.6 13.3 %all-to-all-done.3 = bf16[16,32,512]{2,1,0:T(8,128)(2,1)S(1)} async-done(((bf16[16,32,512]{2,1,0:T(8,128)(2,1)}), bf16[16,32,512]{2,1,0:T(8,128)(2,1)S(1)}, u32[]{:S(2)}, u32[]{:S(2)}) %all-to-all-start.3) | async-done | bytes 524320 | tf_op jit(solution)/shard_map/all_to_all | solution.py:88
  132.9 1.2 gather_fusion.1
  135.5 1.4 multiply_reduce_fusion
  137.7 6.5 %reduce-scatter.2.cloned.1.call-done = bf16[1024,2,512]{2,0,1:T(8,128)(2,1)} async-done(((bf16[2048,2,512]{2,0,1:T(8,128)(2,1)}), bf16[1024,2,512]{2,0,1:T(8,128)(2,1)}) %reduce-scatter.2.cloned.1.call-update) | async-done | bytes 2097168 | tf_op jit(solution)/shard_map/reduce_scatter | solution.py:109
  144.2 3.0 %slice_bitcast_fusion = (bf16[1,1024,512]{2,1,0:T(8,128)(2,1)}, bf16[1,1024,512]{2,1,0:T(8,128)(2,1)}) fusion(bf16[1024,2,512]{2,0,1:T(8,128)(2,1)} %reduce-scatter.2.cloned.1.call-done), kind=kLoop, calls=%fused_computation.26 | loop fusion | bytes 4194304 | tf_op jit(solution)/shard_map/convert_element_type | solution.py:116
  (51 shorter events, 11.3 us)
Async XLA Ops:
  7.2 17.9 %copy-start.3 = (s32[128]{0:T(128)S(1)}, s32[128]{0:T(128)}, u32[]{:S(2)}) copy-start(s32[128]{0:T(128)} %param.12) | copy-start | bytes 1540
  7.2 18.2 %copy-start.1 = (bf16[128,512]{1,0:T(8,128)(2,1)S(1)}, bf16[128,512]{1,0:T(8,128)(2,1)}, u32[]{:S(2)}) copy-start(bf16[128,512]{1,0:T(8,128)(2,1)} %param.15) | copy-start | bytes 393220
  7.2 38.2 %all-gather.3.cloned.1.call-start = ((), (), s32[]{:S(2)}) async-start(), calls=%async_computation.5 | async-start | bytes 3145728 | tf_op jit(solution)/shard_map/all_gather | solution.py:73
  7.9 72.2 %all-gather.5.cloned.1.call-start = ((), (), s32[]{:S(2)}) async-start(), calls=%async_computation.6 | async-start | bytes 3145728 | tf_op jit(solution)/shard_map/all_gather | solution.py:76
  17.7 21.9 %all-to-all-start = ((bf16[16,32,512]{2,1,0:T(8,128)(2,1)}), bf16[16,32,512]{2,1,0:T(8,128)(2,1)S(1)}, u32[]{:S(2)}, u32[]{:S(2)}) async-start(bf16[16,32,512]{2,1,0:T(8,128)(2,1)} %bitcast.7), calls=%async_computation | async-start | bytes 1048576 | tf_op jit(solution)/shard_map/all_to_all | solution.py:69
  39.5 18.6 %all-to-all-start.2 = ((bf16[16,32,512]{2,1,0:T(8,128)(2,1)}), bf16[16,32,512]{2,1,0:T(8,128)(2,1)S(1)}, u32[]{:S(2)}, u32[]{:S(2)}) async-start(bf16[16,32,512]{2,1,0:T(8,128)(2,1)} %bitcast.13), calls=%async_computation.2 | async-start | bytes 1048576 | tf_op jit(solution)/shard_map/all_to_all | solution.py:79
  43.6 100.6 %reduce-scatter.2.cloned.1.call-start = ((), (), s32[]{:S(2)}) async-start(), calls=%async_computation.7 | async-start | bytes 6291456 | tf_op jit(solution)/shard_map/reduce_scatter | solution.py:109
  49.8 36.1 %copy-start.4 = (bf16[512,2048]{1,0:T(8,128)(2,1)}, bf16[512,2048]{1,0:T(8,128)(2,1)S(1)}, u32[]{:S(2)}) copy-start(bf16[512,2048]{1,0:T(8,128)(2,1)S(1)} %get-tuple-element.12) | copy-start | bytes 6291460
  84.5 1.4 copy-start.5
  89.8 10.1 %copy-start.2 = (bf16[1,2048,512]{2,1,0:T(8,128)(2,1)S(1)}, bf16[1,2048,512]{2,1,0:T(8,128)(2,1)}, u32[]{:S(2)}) copy-start(bf16[1,2048,512]{2,1,0:T(8,128)(2,1)} %all-gather.3.cloned.1.call-done) | copy-start | bytes 6291460
  94.2 20.1 %all-to-all-start.1 = ((bf16[16,32,512]{2,1,0:T(8,128)(2,1)}), bf16[16,32,512]{2,1,0:T(8,128)(2,1)S(1)}, u32[]{:S(2)}, u32[]{:S(2)}) async-start(bf16[16,32,512]{2,1,0:T(8,128)(2,1)} %bitcast.11), calls=%async_computation.1 | async-start | bytes 1048576 | tf_op jit(solution)/shard_map/all_to_all | solution.py:78
  103.5 31.9 %copy-start = (bf16[128,512]{1,0:T(8,128)(2,1)S(1)}, bf16[128,512]{1,0:T(8,128)(2,1)}, u32[]{:S(2)}) copy-start(bf16[128,512]{1,0:T(8,128)(2,1)} %param.8) | copy-start | bytes 393220
  114.3 18.6 %all-to-all-start.3 = ((bf16[16,32,512]{2,1,0:T(8,128)(2,1)}), bf16[16,32,512]{2,1,0:T(8,128)(2,1)S(1)}, u32[]{:S(2)}, u32[]{:S(2)}) async-start(bf16[16,32,512]{2,1,0:T(8,128)(2,1)} %bitcast.15), calls=%async_computation.3 | async-start | bytes 1048576 | tf_op jit(solution)/shard_map/all_to_all | solution.py:88
Sparse Core Ops, SparseCore 0:
  9.6 35.8 all-gather.2
  47.0 33.1 all-gather.4
  89.9 54.2 reduce-scatter.1
where the time goes:
time: 154 us
  waiting for transfers between devices  75.3 us (49%)
  starting transfers between devices  21.3 us (14%)
  matrix products  19.5 us (13%)
  between operations  14 us (9%)
  other arithmetic  12 us (8%)
  local copies, waits for them, and re-layouts  11.6 us (8%)
    all_gather x1, waiting for transfers between devices, on_device(): lax.all_gather(down_weight, 'dp', axis=1, tiled=True)[0]  22 us
    dot_general x4, matrix products, row_product(): lax.dot_general(left_side, right_side, numbers, preferred_element_type=jn...  16.9 us
    all_to_all x1, waiting for transfers between devices, on_device(): lax.all_to_all(returning, 'expert', split_axis=0, concat_axis=0, tiled=True)  13.3 us
    all_to_all x1, waiting for transfers between devices, on_device(): lax.all_to_all(send_rows, 'expert', split_axis=0, concat_axis=0, tiled=True)  11.3 us
    all_to_all x1, waiting for transfers between devices, on_device(): lax.all_to_all(outgoing, 'expert', split_axis=0, concat_axis=0, tiled=True)  10.8 us
    all_to_all x1, waiting for transfers between devices, on_device(): lax.all_to_all(send_grad, 'expert', split_axis=0, concat_axis=0, tiled=True)  8.25 us
    all_to_all x1, starting transfers between devices, on_device(): lax.all_to_all(send_rows, 'expert', split_axis=0, concat_axis=0, tiled=True)  7.39 us
    reduce_scatter x1, waiting for transfers between devices, on_device(): lax.psum_scatter((jnp.stack([up_term, down_term], axis=1) * grad_scale).a...  6.51 us
  transfers between devices with their start and end apart: 7, of which 7 were waited for; matrix products, arithmetic and copies ran while one was open for 20% of the time, Pallas kernels for 0%

commit v1 on v0

v1 whole, which is shorter than its diff:
```python
import math

import jax
import jax.numpy as jnp
from jax import lax
from jax.sharding import PartitionSpec as P

root_half = 0.7071067811865476
density = 0.3989422804014327


def product(left_side, right_side, left_axis, right_axis):
    numbers = (((left_axis,), (right_axis,)), ((), ()))
    return lax.dot_general(left_side, right_side, numbers, preferred_element_type=jnp.float32)


def on_device(tokens, modality, modal_gains, routes, gate_share, up_weight, down_weight, cotangent):
    tok_count, width = tokens.shape
    expert_count = lax.axis_size("expert")
    replica_count = lax.axis_size("dp")
    capacity = 4 * tok_count // expert_count
    slot_count = expert_count * capacity
    grad_scale = 1.0 / math.sqrt(2 * tok_count * replica_count)
    up = up_weight[0]
    down = down_weight[0]
    x_float = tokens.astype(jnp.float32)
    inv_rms = lax.rsqrt(jnp.mean(x_float * x_float, axis=-1, keepdims=True) + 1e-06)
    gain_rows = jnp.where(modality[:, None] == 1, modal_gains[1][None, :], modal_gains[0][None, :])
    normed = (x_float * inv_rms * gain_rows).astype(jnp.bfloat16)
    gate_first = gate_share.astype(jnp.float32)[:, None] / 16.0
    column = lax.broadcasted_iota(jnp.int32, (tok_count, slot_count), 1)
    is_first = routes[:, 0:1] == column // capacity
    is_second = routes[:, 1:2] == column // capacity
    named = (is_first | is_second).astype(jnp.bfloat16)
    earlier = (
        lax.broadcasted_iota(jnp.int32, (tok_count, tok_count), 1)
        < lax.broadcasted_iota(jnp.int32, (tok_count, tok_count), 0)
    ).astype(jnp.bfloat16)
    position = product(earlier, named, 1, 0)
    here = (is_first | is_second) & (position == (column % capacity).astype(jnp.float32))
    slot_pick = here.astype(jnp.bfloat16)
    slot_gate = jnp.where(here, jnp.where(is_first, gate_first, 1.0 - gate_first), 0.0).astype(
        jnp.bfloat16
    )
    send = jnp.concatenate(
        [
            product(slot_pick, normed, 0, 0).astype(jnp.bfloat16),
            product(slot_gate, cotangent, 0, 0).astype(jnp.bfloat16),
        ],
        axis=1,
    ).reshape(expert_count, capacity, 2 * width)
    arrived = lax.all_to_all(send, "expert", split_axis=0, concat_axis=0, tiled=True)
    both = lax.all_gather(arrived.reshape(slot_count, 2 * width), "dp", axis=0, tiled=True)
    rows, grads = both[:, :width], both[:, width:]
    pre_act = product(rows, up, 1, 1)
    cdf = 0.5 * (1.0 + lax.erf(pre_act * root_half))
    activated = (pre_act * cdf).astype(jnp.bfloat16)
    hidden_grad = product(grads, down, 1, 1)
    slope = cdf + pre_act * jnp.exp(-0.5 * pre_act * pre_act) * density
    pre_grad = (hidden_grad * slope).astype(jnp.bfloat16)
    parts = jnp.concatenate(
        [
            product(activated, down, 1, 0).astype(jnp.bfloat16),
            product(pre_grad, up, 1, 0).astype(jnp.bfloat16),
        ],
        axis=1,
    )
    summed = lax.psum_scatter(parts, "dp", scatter_dimension=0, tiled=True)
    back = lax.all_to_all(
        summed.reshape(expert_count, capacity, 2 * width),
        "expert",
        split_axis=0,
        concat_axis=0,
        tiled=True,
    ).reshape(slot_count, 2 * width)
    up_grad = (product(pre_grad, rows, 0, 0) * grad_scale).astype(jnp.bfloat16)[None]
    down_grad = (product(activated, grads, 0, 0) * grad_scale).astype(jnp.bfloat16)[None]
    moe_output = product(slot_gate, back[:, :width], 1, 0).astype(jnp.bfloat16)
    scaled = gain_rows * product(slot_pick, back[:, width:], 1, 0)
    token_grad = (
        inv_rms * scaled - x_float * inv_rms**3 * jnp.mean(x_float * scaled, axis=-1, keepdims=True)
    ).astype(jnp.bfloat16)
    return (moe_output, token_grad, up_grad, down_grad)


def solution(mesh):
    token_rows = P(("dp", "expert"), None)
    token_list = P(("dp", "expert"))
    weights = P("expert", "dp", None)
    return jax.shard_map(
        on_device,
        mesh=mesh,
        in_specs=(
            token_rows,
            token_list,
            P(),
            token_rows,
            token_list,
            weights,
            weights,
            token_rows,
        ),
        out_specs=(token_rows, token_rows, weights, weights),
        check_vma=False,
    )
```

time: 154 us -> 163 us (1.058)
  blocking collectives: 0 us -> 32.1 us
  starting transfers between devices: 21.3 us -> 5.7 us
  other arithmetic: 12 us -> 4.83 us
  waiting for transfers between devices: 75.3 us -> 81.9 us
  local copies, waits for them, and re-layouts: 11.6 us -> 5.41 us
  matrix products: 19.5 us -> 17.6 us
    all_to_all x0 -> x1, blocking collectives: none -> 32.1 us  [on_device(): lax.all_to_all(send, 'expert', split_axis=0, concat_axis=0, tiled=True)]
    all_to_all x4 -> x1, waiting for transfers between devices: 43.6 us -> 16.4 us  [on_device(): lax.all_to_all(summed.reshape(expert_count, capacity, 2 * width), 'expert...]
    reduce_scatter x1, waiting for transfers between devices: 6.51 us -> 32 us  [on_device(): summed = lax.psum_scatter(parts, 'dp', scatter_dimension=0, tiled=True)]
    all_to_all x4 -> x1, starting transfers between devices: 21.2 us -> 5.62 us  [on_device(): lax.all_to_all(summed.reshape(expert_count, capacity, 2 * width), 'expert...]
    all_gather x2 -> x1, waiting for transfers between devices: 23.8 us -> 33.5 us  [on_device(): lax.all_gather(arrived.reshape(slot_count, 2 * width), 'dp', axis=0, tile...]
    convert_element_type x3 -> x0, local copies, waits for them, and re-layouts: 3.67 us -> none  [the longest x1 2.99 us: on_device(): down_grad = grad_pair[:, 1][None].astype(jnp.bfloat16)]
    convert_element_type x3 -> x0, other arithmetic: 3.56 us -> none  [the longest x1 2.55 us: on_device(): (jnp.stack([up_term, down_term], axis=1) * grad_scale).astype(jnp.bfloat16)]
    scatter x1 -> x0, other arithmetic: 2.38 us -> none  [on_device(): empty_rows.at[slot_index].set(route_grad)]
  transfers between devices with their start and end apart: 7 -> 3, of which waited for: 7 -> 3; matrix products, arithmetic and copies ran while one was open for 20% -> 4% of each run, Pallas kernels for 0% -> 0%
where the time goes in v1:
time: 163 us; the launch traced here: 162 us
  waiting for transfers between devices  81.9 us (50%)
  blocking collectives  32.1 us (20%)
  matrix products  17.6 us (11%)
  between operations  14.2 us (9%)
  starting transfers between devices  5.7 us (3%)
  local copies, waits for them, and re-layouts  5.41 us (3%)
  other arithmetic  4.83 us (3%)
    all_gather x1, waiting for transfers between devices, on_device(): lax.all_gather(arrived.reshape(slot_count, 2 * width), 'dp', axis=0, tile...  33.5 us
    all_to_all x1, blocking collectives, on_device(): lax.all_to_all(send, 'expert', split_axis=0, concat_axis=0, tiled=True)  32.1 us
    reduce_scatter x1, waiting for transfers between devices, on_device(): summed = lax.psum_scatter(parts, 'dp', scatter_dimension=0, tiled=True)  32 us
    dot_general x11, matrix products, product(): lax.dot_general(left_side, right_side, numbers, preferred_element_type=jn...  17.6 us
    all_to_all x1, waiting for transfers between devices, on_device(): lax.all_to_all(summed.reshape(expert_count, capacity, 2 * width), 'expert...  16.4 us
    all_to_all x1, starting transfers between devices, on_device(): lax.all_to_all(summed.reshape(expert_count, capacity, 2 * width), 'expert...  5.62 us
  transfers between devices with their start and end apart: 3, of which 3 were waited for; matrix products, arithmetic and copies ran while one was open for 4% of the time, Pallas kernels for 0%

profile of v1, /device:TPU:0, one launch (start us, length us, event | category | flops | bytes accessed | tf_op | source)
XLA Modules:
  0.0 161.8 jit_solution(8877882471875722862)
XLA Ops:
  7.3 0.7 broadcast_compare_fusion
  8.0 1.0 fusion.25
  9.0 0.8 slice_bitcast_fusion.1
  9.8 0.7 convert_multiply_fusion.4
  10.5 0.8 fusion.49
  11.5 1.3 convolution_convert_fusion.2
  12.9 0.4 convolution_convert_fusion.3
  13.4 0.5 copy.12
  13.9 32.1 %all_to_all.10 = bf16[16,32,1024]{2,1,0:T(8,128)(2,1)} all-to-all(bf16[16,32,1024]{2,1,0:T(8,128)(2,1)S(1)} %bitcast.34), channel_id=1, replica_groups=mesh['dp'=2,'expert'=16] {'expert'}, dimensions={0} | all-to-all | bytes 2097152 | tf_op jit(solution)/shard_map/all_to_all | solution.py:52
  46.1 33.5 %all-gather.2.cloned.1.call-done = bf16[1024,1024]{1,0:T(8,128)(2,1)} async-done(((bf16[512,1024]{1,0:T(8,128)(2,1)}), bf16[1024,1024]{1,0:T(8,128)(2,1)}) %all-gather.2.cloned.1.call-update) | async-done | bytes 2097168 | tf_op jit(solution)/shard_map/all_gather | solution.py:53
  79.6 2.7 %multiply_convert_fusion = (bf16[1024,1024]{1,0:T(8,128)(2,1)S(1)}, f32[1024,1024]{1,0:T(8,128)S(1)}) fusion(bf16[1,1024,512]{2,1,0:T(8,128)(2,1)S(1)} %copy-done, bf16[1024,1024]{1,0:T(8,128)(2,1)} %all-gather.2.cloned.1.call-done), kind=kOutput, calls=%fused_computation.7 | convolution fusion | flops 1078984704 | bytes 8388608 | tf_op jit(solution)/shard_map/dot_general | solution.py:14
  82.4 1.3 convolution_convert_fusion.1
  83.7 1.0 copy-done.2
  84.7 2.5 %fusion.5 = bf16[1024,1024]{1,0:T(8,128)(2,1)S(1)} fusion(f32[1024,1024]{1,0:T(8,128)S(1)} %get-tuple-element.13, bf16[1,1024,512]{2,1,0:T(8,128)(2,1)S(1)} %copy-done.4, bf16[1024,1024]{1,0:T(8,128)(2,1)S(1)} %copy-done.2), kind=kOutput, calls=%fused_computation.6 | convolution fusion | flops 1084227584 | bytes 8388608 | tf_op jit(solution)/shard_map/dot_general | solution.py:14
  87.2 1.3 convolution_convert_fusion
  88.6 1.5 pad_maximum_fusion
  90.1 32.0 %reduce-scatter.2.cloned.1.call-done = bf16[512,1024]{0,1:T(8,128)(2,1)} async-done(((bf16[1024,1024]{0,1:T(8,128)(2,1)}), bf16[512,1024]{0,1:T(8,128)(2,1)}) %reduce-scatter.2.cloned.1.call-update) | async-done | bytes 1048592 | tf_op jit(solution)/shard_map/reduce_scatter | solution.py:68
  122.1 2.3 %copy.13 = bf16[512,1024]{1,0:T(8,128)(2,1)} copy(bf16[512,1024]{0,1:T(8,128)(2,1)} %reduce-scatter.2.cloned.1.call-done) | data formatting | bytes 2097152 | tf_op jit(solution)/shard_map/reduce_scatter | solution.py:68
  124.4 5.6 %all-to-all-start.1 = ((bf16[16,32,1024]{2,1,0:T(8,128)(2,1)}), bf16[16,32,1024]{2,1,0:T(8,128)(2,1)S(1)}, u32[]{:S(2)}, u32[]{:S(2)}) async-start(bf16[16,32,1024]{2,1,0:T(8,128)(2,1)} %bitcast.8), calls=%async_computation.2 | async-start | bytes 2097152 | tf_op jit(solution)/shard_map/all_to_all | solution.py:69
  130.0 4.3 %fusion.6 = bf16[1,1024,512]{2,1,0:T(8,128)(2,1)} fusion(bf16[1024,1024]{1,0:T(8,128)(2,1)} %copy-done.7, bf16[1024,1024]{1,0:T(8,128)(2,1)} %all-gather.2.cloned.1.call-done), kind=kOutput, calls=%fused_computation.14 | convolution fusion | flops 1074790400 | bytes 4194304 | tf_op jit(solution)/shard_map/dot_general | solution.py:14
  134.3 2.3 %fusion.7 = bf16[1,1024,512]{2,1,0:T(8,128)(2,1)} fusion(bf16[1024,1024]{1,0:T(8,128)(2,1)S(1)} %copy-done.6, bf16[1024,1024]{1,0:T(8,128)(2,1)S(1)} %copy-done.3), kind=kOutput, calls=%fused_computation.15 | convolution fusion | flops 1074790400 | bytes 4194304 | tf_op jit(solution)/shard_map/dot_general | solution.py:14
  136.5 16.4 %all-to-all-done.1 = bf16[16,32,1024]{2,1,0:T(8,128)(2,1)S(1)} async-done(((bf16[16,32,1024]{2,1,0:T(8,128)(2,1)}), bf16[16,32,1024]{2,1,0:T(8,128)(2,1)S(1)}, u32[]{:S(2)}, u32[]{:S(2)}) %all-to-all-start.1) | async-done | bytes 1048608 | tf_op jit(solution)/shard_map/all_to_all | solution.py:69
  152.9 0.9 convolution_convert_fusion.4
  154.2 0.8 fusion.28
  (27 shorter events, 0.9 us)
Async XLA Ops:
  7.2 72.5 %copy-start = (bf16[1,1024,512]{2,1,0:T(8,128)(2,1)S(1)}, bf16[1,1024,512]{2,1,0:T(8,128)(2,1)}, u32[]{:S(2)}) copy-start(bf16[1,1024,512]{2,1,0:T(8,128)(2,1)} %param.13) | copy-start | bytes 3145732
  7.2 5.7 %copy-start.1 = (bf16[128,512]{1,0:T(8,128)(2,1)S(1)}, bf16[128,512]{1,0:T(8,128)(2,1)}, u32[]{:S(2)}) copy-start(bf16[128,512]{1,0:T(8,128)(2,1)} %param.8) | copy-start | bytes 393220
  7.2 72.5 %all-gather.2.cloned.1.call-start = ((), (), s32[]{:S(2)}) async-start(), calls=%async_computation.3 | async-start | bytes 3145728 | tf_op jit(solution)/shard_map/all_gather | solution.py:53
  46.1 36.3 %copy-start.4 = (bf16[1,1024,512]{2,1,0:T(8,128)(2,1)S(1)}, bf16[1,1024,512]{2,1,0:T(8,128)(2,1)}, u32[]{:S(2)}) copy-start(bf16[1,1024,512]{2,1,0:T(8,128)(2,1)} %param.14) | copy-start | bytes 3145732
  46.1 76.0 %reduce-scatter.2.cloned.1.call-start = ((), (), s32[]{:S(2)}) async-start(), calls=%async_computation.4 | async-start | bytes 3145728 | tf_op jit(solution)/shard_map/reduce_scatter | solution.py:68
  82.4 1.4 copy-start.5
  82.4 2.3 %copy-start.2 = (bf16[1024,1024]{1,0:T(8,128)(2,1)S(1)}, bf16[1024,1024]{1,0:T(8,128)(2,1)}, u32[]{:S(2)}) copy-start(bf16[1024,1024]{1,0:T(8,128)(2,1)} %all-gather.2.cloned.1.call-done) | copy-start | bytes 6291460
  87.2 1.4 copy-start.7
  124.4 28.6 %all-to-all-start.1 = ((bf16[16,32,1024]{2,1,0:T(8,128)(2,1)}), bf16[16,32,1024]{2,1,0:T(8,128)(2,1)S(1)}, u32[]{:S(2)}, u32[]{:S(2)}) async-start(bf16[16,32,1024]{2,1,0:T(8,128)(2,1)} %bitcast.8), calls=%async_computation.2 | async-start | bytes 2097152 | tf_op jit(solution)/shard_map/all_to_all | solution.py:69
  130.0 4.3 %copy-start.3 = (bf16[1024,1024]{1,0:T(8,128)(2,1)S(1)}, bf16[1024,1024]{1,0:T(8,128)(2,1)}, u32[]{:S(2)}) copy-start(bf16[1024,1024]{1,0:T(8,128)(2,1)} %all-gather.2.cloned.1.call-done) | copy-start | bytes 6291460
  130.0 4.3 %copy-start.6 = (bf16[1024,1024]{1,0:T(8,128)(2,1)S(1)}, bf16[1024,1024]{1,0:T(8,128)(2,1)}, u32[]{:S(2)}) copy-start(bf16[1024,1024]{1,0:T(8,128)(2,1)} %copy-done.5) | copy-start | bytes 6291460
Sparse Core Ops, SparseCore 0:
  46.2 33.4 all-gather.1
  90.2 31.8 reduce-scatter.1

commit v2 on v1

v2 whole, which is shorter than its diff:
```python
import functools
import math

import jax
import jax.numpy as jnp
from jax import lax
from jax.experimental import pallas as pl
from jax.experimental.pallas import tpu as pltpu
from jax.sharding import PartitionSpec as P

root_half = 0.7071067811865476
density = 0.3989422804014327
MESH = pl.DeviceIdType.MESH


def product(left_side, right_side, left_axis, right_axis):
    numbers = (((left_axis,), (right_axis,)), ((), ()))
    return lax.dot_general(left_side, right_side, numbers, preferred_element_type=jnp.float32)


def layer_kernel(
    experts,
    replicas,
    chunks,
    tokens,
    modality,
    gains,
    routes,
    gate_share,
    up,
    down,
    cotangent,
    moe_output,
    token_grad,
    up_grad,
    down_grad,
    send,
    recv,
    parts,
    part_recv,
    own,
    outgoing,
    back,
    act,
    pre_grad,
    slot_pick,
    slot_gate,
    in_send,
    in_recv,
    fwd_send,
    fwd_recv,
    part_send_sem,
    part_recv_sem,
    back_send,
    back_recv,
):
    me = lax.axis_index("expert")
    dp = lax.axis_index("dp")
    tok_count, width = tokens.shape
    capacity = send.shape[1]
    slot_count = experts * capacity
    group = experts // chunks
    chunk_rows = group * capacity
    hidden = up.shape[0]
    hidden_tile = min(256, hidden)
    grad_scale = 1.0 / math.sqrt(2 * tok_count * replicas)
    bits = experts.bit_length() - 1

    def peer(offset):
        total = 0
        for bit in range(bits):
            unit = 1 << bit
            total = total + ((me // unit + offset // unit) % 2) * unit
        return total

    def in_copy(s):
        return pltpu.make_async_remote_copy(
            src_ref=send.at[s],
            dst_ref=recv.at[0, s],
            send_sem=in_send.at[s],
            recv_sem=in_recv.at[s],
            device_id={"expert": peer(s)},
            device_id_type=MESH,
        )

    def back_copy(s):
        return pltpu.make_async_remote_copy(
            src_ref=outgoing.at[s],
            dst_ref=back.at[s],
            send_sem=back_send.at[s],
            recv_sem=back_recv.at[s],
            device_id={"expert": peer(s)},
            device_id_type=MESH,
        )

    def fwd_copy(q, c):
        span = pl.ds(c * group, group)
        return pltpu.make_async_remote_copy(
            src_ref=recv.at[0, span],
            dst_ref=recv.at[q, span],
            send_sem=fwd_send.at[q - 1, c],
            recv_sem=fwd_recv.at[q - 1, c],
            device_id={"dp": (dp + q) % replicas},
            device_id_type=MESH,
        )

    def part_copy(q, c):
        span = pl.ds(c * group, group)
        return pltpu.make_async_remote_copy(
            src_ref=parts.at[q - 1, span],
            dst_ref=part_recv.at[q - 1, span],
            send_sem=part_send_sem.at[q - 1, c],
            recv_sem=part_recv_sem.at[q - 1, c],
            device_id={"dp": (dp + replicas - q) % replicas},
            device_id_type=MESH,
        )

    barrier = pltpu.get_barrier_semaphore()

    @pl.loop(1, experts)
    def _(s):
        pl.semaphore_signal(barrier, inc=1, device_id={"expert": peer(s)}, device_id_type=MESH)

    for q in range(1, replicas):
        pl.semaphore_signal(
            barrier, inc=1, device_id={"dp": (dp + q) % replicas}, device_id_type=MESH
        )

    def norm_parts():
        x_float = tokens[...].astype(jnp.float32)
        inv_rms = lax.rsqrt(jnp.mean(x_float * x_float, axis=-1, keepdims=True) + 1e-06)
        is_text = jnp.broadcast_to(modality[...], (tok_count, width)) == 1
        gain_rows = jnp.where(is_text, gains[1:2, :], gains[0:1, :])
        return x_float, inv_rms, gain_rows

    x_float, inv_rms, gain_rows = norm_parts()
    normed = (x_float * inv_rms * gain_rows).astype(jnp.bfloat16)
    column = lax.broadcasted_iota(jnp.int32, (tok_count, slot_count), 1)
    column_expert = (column // capacity) ^ me
    is_first = jnp.broadcast_to(routes[:, 0:1], column.shape) == column_expert
    is_second = jnp.broadcast_to(routes[:, 1:2], column.shape) == column_expert
    named = jnp.where(is_first | is_second, 1.0, 0.0)
    earlier = jnp.where(
        lax.broadcasted_iota(jnp.int32, (tok_count, tok_count), 1)
        < lax.broadcasted_iota(jnp.int32, (tok_count, tok_count), 0),
        1.0,
        0.0,
    )
    position = product(earlier.astype(jnp.bfloat16), named.astype(jnp.bfloat16), 1, 0)
    place = (column % capacity).astype(jnp.float32)
    pick = jnp.where(position == place, named, 0.0)
    first = jnp.broadcast_to(gate_share[...].astype(jnp.float32) / 16.0, column.shape)
    gate = pick * jnp.where(is_first, first, 1.0 - first)
    slot_pick[...] = pick.astype(jnp.bfloat16)
    slot_gate[...] = gate.astype(jnp.bfloat16)
    send[:, :, :width] = (
        product(slot_pick[...], normed, 0, 0)
        .reshape(experts, capacity, width)
        .astype(jnp.bfloat16)
    )
    send[:, :, width:] = (
        product(slot_gate[...], cotangent[...], 0, 0)
        .reshape(experts, capacity, width)
        .astype(jnp.bfloat16)
    )

    pl.semaphore_wait(barrier, experts + replicas - 2)

    @pl.loop(1, experts)
    def _(s):
        in_copy(s).start()

    recv[0, 0] = send[0]

    def take_in(c):
        for j in range(group):
            s = c * group + j
            if j == 0:

                @pl.when(c > 0)
                def _():
                    in_copy(s).wait_recv()
            else:
                in_copy(s).wait_recv()
        for q in range(1, replicas):
            fwd_copy(q, c).start()

    def work(c):
        span = pl.ds(c * group, group)
        place_rows = pl.ds(pl.multiple_of(c * chunk_rows, chunk_rows), chunk_rows)
        for q in range(1, replicas):
            fwd_copy(q, c).wait_recv()

        def gathered(low):
            return jnp.concatenate(
                [
                    recv[q, span, :, low : low + width].reshape(chunk_rows, width)
                    for q in range(replicas)
                ],
                axis=0,
            )

        rows, grads = gathered(0), gathered(width)
        for low in range(0, hidden, hidden_tile):
            high = low + hidden_tile
            pre_act = product(rows, up[low:high, :], 1, 1)
            hidden_grad = product(grads, down[low:high, :], 1, 1)
            cdf = 0.5 * (1.0 + lax.erf(pre_act * root_half))
            activated = (pre_act * cdf).astype(jnp.bfloat16)
            slope = cdf + pre_act * jnp.exp(-0.5 * pre_act * pre_act) * density
            grad = (hidden_grad * slope).astype(jnp.bfloat16)
            for q in range(replicas):
                part = slice(q * chunk_rows, (q + 1) * chunk_rows)
                act[q, place_rows, low:high] = activated[part]
                pre_grad[q, place_rows, low:high] = grad[part]

        for store, weight, low in ((act, down, 0), (pre_grad, up, width)):
            values = jnp.concatenate([store[q, place_rows, :] for q in range(replicas)], axis=0)
            result = product(values, weight[...], 1, 0)
            own[place_rows, low : low + width] = result[:chunk_rows]
            for q in range(1, replicas):
                part = result[q * chunk_rows : (q + 1) * chunk_rows]
                parts[q - 1, span, :, low : low + width] = part.reshape(
                    group, capacity, width
                ).astype(jnp.bfloat16)
        for q in range(1, replicas):
            part_copy(q, c).start()

    def give_back(c):
        span = pl.ds(c * group, group)
        place_rows = pl.ds(pl.multiple_of(c * chunk_rows, chunk_rows), chunk_rows)
        for q in range(1, replicas):
            part_copy(q, c).wait_recv()
        total = own[place_rows, :].reshape(group, capacity, 2 * width)
        for q in range(1, replicas):
            total = total + part_recv[q - 1, span].astype(jnp.float32)
        outgoing[span] = total.astype(jnp.bfloat16)
        for j in range(group):
            s = c * group + j
            if j == 0:

                @pl.when(c > 0)
                def _():
                    back_copy(s).start()
            else:
                back_copy(s).start()

    @pl.loop(0, chunks + 2)
    def _(t):
        @pl.when(t < chunks)
        def _():
            take_in(t)

        @pl.when((t >= 1) & (t < chunks + 1))
        def _():
            work(t - 1)

        @pl.when(t >= 2)
        def _():
            give_back(t - 2)

    back[0] = outgoing[0]

    for low in range(0, hidden, hidden_tile):
        high = low + hidden_tile
        for store, target, left in ((pre_grad, up_grad, 0), (act, down_grad, width)):
            total = 0.0
            for q in range(replicas):
                rows = recv[q, :, :, left : left + width].reshape(slot_count, width)
                total = total + product(store[q, :, low:high], rows, 0, 0)
            target[low:high, :] = (total * grad_scale).astype(jnp.bfloat16)

    @pl.loop(1, experts)
    def _(s):
        back_copy(s).wait_recv()

    returned = back[:, :, :width].reshape(slot_count, width)
    moe_output[...] = product(slot_gate[...], returned, 1, 0).astype(jnp.bfloat16)
    x_float, inv_rms, gain_rows = norm_parts()
    returned = back[:, :, width:].reshape(slot_count, width)
    scaled = gain_rows * product(slot_pick[...], returned, 1, 0)
    inner = jnp.mean(x_float * scaled, axis=-1, keepdims=True)
    token_grad[...] = (
        inv_rms * scaled - x_float * (inv_rms * inv_rms * inv_rms) * inner
    ).astype(jnp.bfloat16)

    @pl.loop(1, experts)
    def _(s):
        in_copy(s).wait_send()
        back_copy(s).wait_send()

    @pl.loop(0, chunks)
    def _(c):
        for q in range(1, replicas):
            fwd_copy(q, c).wait_send()
            part_copy(q, c).wait_send()


def on_device(tokens, modality, modal_gains, routes, gate_share, up_weight, down_weight, cotangent):
    tok_count, width = tokens.shape
    experts = lax.axis_size("expert")
    replicas = lax.axis_size("dp")
    capacity = 4 * tok_count // experts
    slots = experts * capacity
    hidden = up_weight.shape[1]
    chunks = 4
    half = jnp.bfloat16
    blocks = (experts, capacity, 2 * width)
    dma = pltpu.SemaphoreType.DMA
    in_vmem = pl.BlockSpec(memory_space=pltpu.VMEM)
    moe_output, token_grad, up_grad, down_grad = pl.pallas_call(
        functools.partial(layer_kernel, experts, replicas, chunks),
        out_shape=(
            jax.ShapeDtypeStruct((tok_count, width), half),
            jax.ShapeDtypeStruct((tok_count, width), half),
            jax.ShapeDtypeStruct((hidden, width), half),
            jax.ShapeDtypeStruct((hidden, width), half),
        ),
        in_specs=[in_vmem] * 8,
        out_specs=(in_vmem,) * 4,
        scratch_shapes=[
            pltpu.VMEM(blocks, half),
            pltpu.VMEM((replicas,) + blocks, half),
            pltpu.VMEM((replicas - 1,) + blocks, half),
            pltpu.VMEM((replicas - 1,) + blocks, half),
            pltpu.VMEM((slots, 2 * width), jnp.float32),
            pltpu.VMEM(blocks, half),
            pltpu.VMEM(blocks, half),
            pltpu.VMEM((replicas, slots, hidden), half),
            pltpu.VMEM((replicas, slots, hidden), half),
            pltpu.VMEM((tok_count, slots), half),
            pltpu.VMEM((tok_count, slots), half),
            dma((experts,)),
            dma((experts,)),
            dma((replicas - 1, chunks)),
            dma((replicas - 1, chunks)),
            dma((replicas - 1, chunks)),
            dma((replicas - 1, chunks)),
            dma((experts,)),
            dma((experts,)),
        ],
        compiler_params=pltpu.CompilerParams(
            collective_id=0, has_side_effects=True, vmem_limit_bytes=56 * 1024 * 1024
        ),
    )(
        tokens,
        modality[:, None],
        modal_gains,
        routes,
        gate_share[:, None],
        up_weight[0],
        down_weight[0],
        cotangent,
    )
    return (moe_output, token_grad, up_grad[None], down_grad[None])


def solution(mesh):
    token_rows = P(("dp", "expert"), None)
    token_list = P(("dp", "expert"))
    weights = P("expert", "dp", None)
    return jax.shard_map(
        on_device,
        mesh=mesh,
        in_specs=(
            token_rows,
            token_list,
            P(),
            token_rows,
            token_list,
            weights,
            weights,
            token_rows,
        ),
        out_specs=(token_rows, token_rows, weights, weights),
        check_vma=False,
    )
```

time: 163 us -> 88.5 us (0.54)
  the two profiles are of different devices: /device:TPU:0 before, /device:TPU:9 now
where the time goes in v2:
time: 88.5 us; the launch traced here: 88.3 us
  Pallas kernels  79.2 us (89%)
  local copies, waits for them, and re-layouts  8.46 us (10%)
    pallas_call x1, Pallas kernels, on_device(): pl.pallas_call(functools.partial(layer_kernel, experts, replicas, chunks)...  79.2 us
    unnamed x15, local copies, waits for them, and re-layouts  6.98 us

profile of v2, /device:TPU:9, one launch (start us, length us, event | category | flops | bytes accessed | tf_op | source)
XLA Modules:
  0.0 88.3 jit_solution(6493052419299068639)
XLA Ops:
  0.6 0.0 copy-start.3
  0.6 0.6 copy-done.3
  1.3 0.0 copy-start.2
  1.3 0.7 copy.12.modality
  2.0 0.0 copy-done.2
  2.0 0.0 copy-start.4
  2.0 0.7 copy.13.routes
  2.8 0.0 copy-done.4
  2.8 0.7 copy.14.gate_share
  3.5 79.2 %shard_map.111 = (bf16[128,512]{1,0:T(8,128)(2,1)}, bf16[128,512]{1,0:T(8,128)(2,1)}, bf16[1024,512]{1,0:T(8,128)(2,1)}, bf16[1024,512]{1,0:T(8,128)(2,1)}) custom-call(bf16[128,512]{1,0:T(8,128)(2,1)} %tokens.1, s32[128,1]{1,0:T(8,128)} %copy.12.modality, f32[2,512]{1,0:T(2,128)} %gains.1, s32[128,2]{1,0:T(8,128)} %copy.13.routes, ...), custom_call_target="tpu_custom_call" | custom-call | tf_op jit(solution)/shard_map/pallas_call | solution.py:311
  82.7 0.0 copy-start.1
  82.7 1.6 %copy.19 = bf16[128,512]{1,0:T(8,128)(2,1)} copy(bf16[128,512]{1,0:T(8,128)(2,1)} %get-tuple-element.16) | data formatting | bytes 262144
  84.3 0.0 copy-done.1
  84.3 0.7 copy.20
  85.0 0.0 copy-start
  85.0 2.4 %copy.21 = bf16[1,1024,512]{2,1,0:T(8,128)(2,1)} copy(bf16[1,1024,512]{2,1,0:T(8,128)(2,1)} %bitcast.9) | data formatting | bytes 2097152
  87.4 0.0 copy-done
  87.4 1.0 %copy.22 = bf16[1,1024,512]{2,1,0:T(8,128)(2,1)} copy(bf16[1,1024,512]{2,1,0:T(8,128)(2,1)S(1)} %bitcast.8) | data formatting | bytes 2097152
Async XLA Ops:
  0.6 0.7 copy-start.3
  1.3 0.7 copy-start.2
  2.0 0.7 copy-start.4
  82.7 1.6 %copy-start.1 = (bf16[128,512]{1,0:T(8,128)(2,1)S(1)}, bf16[128,512]{1,0:T(8,128)(2,1)}, u32[]{:S(2)}) copy-start(bf16[128,512]{1,0:T(8,128)(2,1)} %get-tuple-element.17) | copy-start | bytes 393220
  85.0 2.4 %copy-start = (bf16[1024,512]{1,0:T(8,128)(2,1)S(1)}, bf16[1024,512]{1,0:T(8,128)(2,1)}, u32[]{:S(2)}) copy-start(bf16[1024,512]{1,0:T(8,128)(2,1)} %get-tuple-element.11) | copy-start | bytes 3145732

commit v3 on v2

--- a/solution.py
+++ b/solution.py
@@ -73,6 +73,19 @@
             total = total + ((me // unit + offset // unit) % 2) * unit
         return total
 
+    def turn(t):
+        step = t // (chunks // 4)
+        return (2 * step + 3 * (step // 2)) % 4 * (chunks // 4) + t % (chunks // 4)
+
+    def unless_own(c, j, act_on):
+        if j == 0:
+
+            @pl.when(c > 0)
+            def _():
+                act_on(c * group)
+        else:
+            act_on(c * group + j)
+
     def in_copy(s):
         return pltpu.make_async_remote_copy(
             src_ref=send.at[s],
@@ -126,10 +139,15 @@
             barrier, inc=1, device_id={"dp": (dp + q) % replicas}, device_id_type=MESH
         )
 
+    marks = jnp.concatenate(
+        [modality[...], routes[...], gate_share[...], jnp.zeros((4, tok_count), jnp.int32)], axis=0
+    )
+    marks = marks.astype(jnp.float32).T.astype(jnp.int32)
+
     def norm_parts():
         x_float = tokens[...].astype(jnp.float32)
         inv_rms = lax.rsqrt(jnp.mean(x_float * x_float, axis=-1, keepdims=True) + 1e-06)
-        is_text = jnp.broadcast_to(modality[...], (tok_count, width)) == 1
+        is_text = jnp.broadcast_to(marks[:, 0:1], (tok_count, width)) == 1
         gain_rows = jnp.where(is_text, gains[1:2, :], gains[0:1, :])
         return x_float, inv_rms, gain_rows
 
@@ -137,8 +155,8 @@
     normed = (x_float * inv_rms * gain_rows).astype(jnp.bfloat16)
     column = lax.broadcasted_iota(jnp.int32, (tok_count, slot_count), 1)
     column_expert = (column // capacity) ^ me
-    is_first = jnp.broadcast_to(routes[:, 0:1], column.shape) == column_expert
-    is_second = jnp.broadcast_to(routes[:, 1:2], column.shape) == column_expert
+    is_first = jnp.broadcast_to(marks[:, 1:2], column.shape) == column_expert
+    is_second = jnp.broadcast_to(marks[:, 2:3], column.shape) == column_expert
     named = jnp.where(is_first | is_second, 1.0, 0.0)
     earlier = jnp.where(
         lax.broadcasted_iota(jnp.int32, (tok_count, tok_count), 1)
@@ -149,7 +167,7 @@
     position = product(earlier.astype(jnp.bfloat16), named.astype(jnp.bfloat16), 1, 0)
     place = (column % capacity).astype(jnp.float32)
     pick = jnp.where(position == place, named, 0.0)
-    first = jnp.broadcast_to(gate_share[...].astype(jnp.float32) / 16.0, column.shape)
+    first = jnp.broadcast_to(marks[:, 3:4].astype(jnp.float32) / 16.0, column.shape)
     gate = pick * jnp.where(is_first, first, 1.0 - first)
     slot_pick[...] = pick.astype(jnp.bfloat16)
     slot_gate[...] = gate.astype(jnp.bfloat16)
@@ -166,22 +184,17 @@
 
     pl.semaphore_wait(barrier, experts + replicas - 2)
 
-    @pl.loop(1, experts)
-    def _(s):
-        in_copy(s).start()
-
     recv[0, 0] = send[0]
+
+    @pl.loop(0, chunks)
+    def _(t):
+        c = turn(t)
+        for j in range(group):
+            unless_own(c, j, lambda s: in_copy(s).start())
 
     def take_in(c):
         for j in range(group):
-            s = c * group + j
-            if j == 0:
-
-                @pl.when(c > 0)
-                def _():
-                    in_copy(s).wait_recv()
-            else:
-                in_copy(s).wait_recv()
+            unless_own(c, j, lambda s: in_copy(s).wait_recv())
         for q in range(1, replicas):
             fwd_copy(q, c).start()
 
@@ -236,28 +249,21 @@
             total = total + part_recv[q - 1, span].astype(jnp.float32)
         outgoing[span] = total.astype(jnp.bfloat16)
         for j in range(group):
-            s = c * group + j
-            if j == 0:
-
-                @pl.when(c > 0)
-                def _():
-                    back_copy(s).start()
-            else:
-                back_copy(s).start()
+            unless_own(c, j, lambda s: back_copy(s).start())
 
     @pl.loop(0, chunks + 2)
     def _(t):
         @pl.when(t < chunks)
         def _():
-            take_in(t)
+            take_in(turn(t))
 
         @pl.when((t >= 1) & (t < chunks + 1))
         def _():
-            work(t - 1)
+            work(turn(t - 1))
 
         @pl.when(t >= 2)
         def _():
-            give_back(t - 2)
+            give_back(turn(t - 2))
 
     back[0] = outgoing[0]
 
@@ -303,7 +309,7 @@
     capacity = 4 * tok_count // experts
     slots = experts * capacity
     hidden = up_weight.shape[1]
-    chunks = 4
+    chunks = 8
     half = jnp.bfloat16
     blocks = (experts, capacity, 2 * width)
     dma = pltpu.SemaphoreType.DMA
@@ -344,10 +350,10 @@
         ),
     )(
         tokens,
-        modality[:, None],
+        modality[None],
         modal_gains,
-        routes,
-        gate_share[:, None],
+        routes.T,
+        gate_share[None],
         up_weight[0],
         down_weight[0],
         cotangent,

time: 88.5 us -> 74.3 us (0.84)
  the two profiles are of different devices: /device:TPU:9 before, /device:TPU:0 now
where the time goes in v3:
time: 74.3 us; the launch traced here: 73.9 us
  Pallas kernels  67.7 us (91%)
  local copies, waits for them, and re-layouts  5.59 us (8%)
    pallas_call x1, Pallas kernels, on_device(): pl.pallas_call(functools.partial(layer_kernel, experts, replicas, chunks)...  67.7 us
    unnamed x8, local copies, waits for them, and re-layouts  5.59 us

profile of v3, /device:TPU:0, one launch (start us, length us, event | category | flops | bytes accessed | tf_op | source)
XLA Modules:
  0.0 73.9 jit_solution(8625131987786906471)
XLA Ops:
  0.6 67.7 %shard_map.111 = (bf16[128,512]{1,0:T(8,128)(2,1)}, bf16[128,512]{1,0:T(8,128)(2,1)}, bf16[1024,512]{1,0:T(8,128)(2,1)}, bf16[1024,512]{1,0:T(8,128)(2,1)}) custom-call(bf16[128,512]{1,0:T(8,128)(2,1)} %tokens.1, s32[1,128]{1,0:T(1,128)} %bitcast.12, f32[2,512]{1,0:T(2,128)} %gains.1, s32[2,128]{1,0:T(2,128)} %bitcast.11, s32[1,128]{1,0:T(1,128)} %bitcast.13, ...), custom_call_target="tpu_custom_call" | custom-call | tf_op jit(solution)/shard_map/pallas_call | solution.py:317
  68.3 0.0 copy-start.1
  68.3 1.6 %copy.16 = bf16[128,512]{1,0:T(8,128)(2,1)} copy(bf16[128,512]{1,0:T(8,128)(2,1)} %get-tuple-element.16) | data formatting | bytes 262144
  69.9 0.0 copy-done.1
  69.9 0.7 copy.17
  70.6 0.0 copy-start
  70.6 2.4 %copy.18 = bf16[1,1024,512]{2,1,0:T(8,128)(2,1)} copy(bf16[1,1024,512]{2,1,0:T(8,128)(2,1)} %bitcast.8) | data formatting | bytes 2097152
  73.0 0.0 copy-done
  73.0 1.0 %copy.19 = bf16[1,1024,512]{2,1,0:T(8,128)(2,1)} copy(bf16[1,1024,512]{2,1,0:T(8,128)(2,1)S(1)} %bitcast.7) | data formatting | bytes 2097152
Async XLA Ops:
  68.3 1.6 %copy-start.1 = (bf16[128,512]{1,0:T(8,128)(2,1)S(1)}, bf16[128,512]{1,0:T(8,128)(2,1)}, u32[]{:S(2)}) copy-start(bf16[128,512]{1,0:T(8,128)(2,1)} %get-tuple-element.17) | copy-start | bytes 393220
  70.6 2.4 %copy-start = (bf16[1024,512]{1,0:T(8,128)(2,1)S(1)}, bf16[1024,512]{1,0:T(8,128)(2,1)}, u32[]{:S(2)}) copy-start(bf16[1024,512]{1,0:T(8,128)(2,1)} %get-tuple-element.11) | copy-start | bytes 3145732

commit v4 on v3

--- a/solution.py
+++ b/solution.py
@@ -53,6 +53,21 @@
     part_recv_sem,
     back_send,
     back_recv,
+    marks_out,
+    marks_in,
+    dense_out,
+    dense_in,
+    near_send,
+    near_back,
+    sums_out,
+    sums_in,
+    other_pick,
+    other_gate,
+    dense_sems,
+    marks_sems,
+    sums_sems,
+    near_sems,
+    return_sems,
 ):
     me = lax.axis_index("expert")
     dp = lax.axis_index("dp")
@@ -74,8 +89,9 @@
         return total
 
     def turn(t):
-        step = t // (chunks // 4)
-        return (2 * step + 3 * (step // 2)) % 4 * (chunks // 4) + t % (chunks // 4)
+        step = (t // (chunks // 4) + 3) % 4
+        quarter = step // 2 * 2 + (step % 2 + step // 2) % 2
+        return quarter * (chunks // 4) + t % (chunks // 4)
 
     def unless_own(c, j, act_on):
         if j == 0:
@@ -106,6 +122,45 @@
             device_id_type=MESH,
         )
 
+    def over_dp(source, target, sems, q, step):
+        return pltpu.make_async_remote_copy(
+            src_ref=source,
+            dst_ref=target.at[q - 1],
+            send_sem=sems.at[0, q - 1],
+            recv_sem=sems.at[1, q - 1],
+            device_id={"dp": (dp + step) % replicas},
+            device_id_type=MESH,
+        )
+
+    def dense_copy(q):
+        return over_dp(dense_out, dense_in, dense_sems, q, q)
+
+    def marks_copy(q):
+        return over_dp(marks_out, marks_in, marks_sems, q, q)
+
+    def sums_copy(q):
+        return over_dp(sums_out.at[q - 1], sums_in, sums_sems, q, replicas - q)
+
+    def near_copy(q, s):
+        return pltpu.make_async_remote_copy(
+            src_ref=near_send.at[q - 1, s],
+            dst_ref=recv.at[q, s],
+            send_sem=near_sems.at[0, q - 1, s],
+            recv_sem=near_sems.at[1, q - 1, s],
+            device_id={"expert": peer(s)},
+            device_id_type=MESH,
+        )
+
+    def return_copy(q, s):
+        return pltpu.make_async_remote_copy(
+            src_ref=parts.at[q - 1, s],
+            dst_ref=near_back.at[q - 1, s],
+            send_sem=return_sems.at[0, q - 1, s],
+            recv_sem=return_sems.at[1, q - 1, s],
+            device_id={"expert": peer(s)},
+            device_id_type=MESH,
+        )
+
     def fwd_copy(q, c):
         span = pl.ds(c * group, group)
         return pltpu.make_async_remote_copy(
@@ -139,10 +194,10 @@
             barrier, inc=1, device_id={"dp": (dp + q) % replicas}, device_id_type=MESH
         )
 
-    marks = jnp.concatenate(
+    marks_out[...] = jnp.concatenate(
         [modality[...], routes[...], gate_share[...], jnp.zeros((4, tok_count), jnp.int32)], axis=0
     )
-    marks = marks.astype(jnp.float32).T.astype(jnp.int32)
+    marks = marks_out[...].astype(jnp.float32).T.astype(jnp.int32)
 
     def norm_parts():
         x_float = tokens[...].astype(jnp.float32)
@@ -153,36 +208,39 @@
 
     x_float, inv_rms, gain_rows = norm_parts()
     normed = (x_float * inv_rms * gain_rows).astype(jnp.bfloat16)
-    column = lax.broadcasted_iota(jnp.int32, (tok_count, slot_count), 1)
-    column_expert = (column // capacity) ^ me
-    is_first = jnp.broadcast_to(marks[:, 1:2], column.shape) == column_expert
-    is_second = jnp.broadcast_to(marks[:, 2:3], column.shape) == column_expert
-    named = jnp.where(is_first | is_second, 1.0, 0.0)
-    earlier = jnp.where(
-        lax.broadcasted_iota(jnp.int32, (tok_count, tok_count), 1)
-        < lax.broadcasted_iota(jnp.int32, (tok_count, tok_count), 0),
-        1.0,
-        0.0,
-    )
-    position = product(earlier.astype(jnp.bfloat16), named.astype(jnp.bfloat16), 1, 0)
-    place = (column % capacity).astype(jnp.float32)
-    pick = jnp.where(position == place, named, 0.0)
-    first = jnp.broadcast_to(marks[:, 3:4].astype(jnp.float32) / 16.0, column.shape)
-    gate = pick * jnp.where(is_first, first, 1.0 - first)
-    slot_pick[...] = pick.astype(jnp.bfloat16)
-    slot_gate[...] = gate.astype(jnp.bfloat16)
-    send[:, :, :width] = (
-        product(slot_pick[...], normed, 0, 0)
-        .reshape(experts, capacity, width)
-        .astype(jnp.bfloat16)
-    )
-    send[:, :, width:] = (
-        product(slot_gate[...], cotangent[...], 0, 0)
-        .reshape(experts, capacity, width)
-        .astype(jnp.bfloat16)
-    )
-
+    dense_out[:, :width] = normed
+    dense_out[:, width:] = cotangent[...]
     pl.semaphore_wait(barrier, experts + replicas - 2)
+    for q in range(1, replicas):
+        marks_copy(q).start()
+        dense_copy(q).start()
+
+    def slots_of(numbers, columns):
+        column = lax.broadcasted_iota(jnp.int32, (tok_count, columns), 1)
+        column_expert = (column // capacity) ^ me
+        is_first = jnp.broadcast_to(numbers[:, 1:2], column.shape) == column_expert
+        is_second = jnp.broadcast_to(numbers[:, 2:3], column.shape) == column_expert
+        named = jnp.where(is_first | is_second, 1.0, 0.0)
+        earlier = jnp.where(
+            lax.broadcasted_iota(jnp.int32, (tok_count, tok_count), 1)
+            < lax.broadcasted_iota(jnp.int32, (tok_count, tok_count), 0),
+            1.0,
+            0.0,
+        )
+        position = product(earlier.astype(jnp.bfloat16), named.astype(jnp.bfloat16), 1, 0)
+        place = (column % capacity).astype(jnp.float32)
+        pick = jnp.where(position == place, named, 0.0)
+        first = jnp.broadcast_to(numbers[:, 3:4].astype(jnp.float32) / 16.0, column.shape)
+        gate = pick * jnp.where(is_first, first, 1.0 - first)
+        return pick.astype(jnp.bfloat16), gate.astype(jnp.bfloat16)
+
+    def slot_blocks(chosen, values):
+        blocks = product(chosen, values, 0, 0).astype(jnp.bfloat16)
+        return blocks.reshape(-1, capacity, width)
+
+    slot_pick[...], slot_gate[...] = slots_of(marks, slot_count)
+    send[:, :, :width] = slot_blocks(slot_pick[...], normed)
+    send[:, :, width:] = slot_blocks(slot_gate[...], cotangent[...])
 
     recv[0, 0] = send[0]
 
@@ -192,17 +250,46 @@
         for j in range(group):
             unless_own(c, j, lambda s: in_copy(s).start())
 
+    near = experts // 2
+    near_chunks = chunks // 2
+    for q in range(1, replicas):
+        marks_copy(q).wait_recv()
+        numbers = marks_in[q - 1].astype(jnp.float32).T.astype(jnp.int32)
+        pick, gate = slots_of(numbers, near * capacity)
+        other_pick[q - 1] = pick
+        other_gate[q - 1] = gate
+        dense_copy(q).wait_recv()
+        near_send[q - 1, :, :, :width] = slot_blocks(pick, dense_in[q - 1, :, :width])
+        near_send[q - 1, :, :, width:] = slot_blocks(gate, dense_in[q - 1, :, width:])
+        recv[q, 0] = near_send[q - 1, 0]
+
+        @pl.loop(1, near)
+        def _(s):
+            near_copy(q, s).start()
+
     def take_in(c):
         for j in range(group):
             unless_own(c, j, lambda s: in_copy(s).wait_recv())
-        for q in range(1, replicas):
-            fwd_copy(q, c).start()
+
+        @pl.when(c >= near_chunks)
+        def _():
+            for q in range(1, replicas):
+                fwd_copy(q, c).start()
 
     def work(c):
         span = pl.ds(c * group, group)
         place_rows = pl.ds(pl.multiple_of(c * chunk_rows, chunk_rows), chunk_rows)
-        for q in range(1, replicas):
-            fwd_copy(q, c).wait_recv()
+
+        @pl.when(c >= near_chunks)
+        def _():
+            for q in range(1, replicas):
+                fwd_copy(q, c).wait_recv()
+
+        @pl.when(c < near_chunks)
+        def _():
+            for q in range(1, replicas):
+                for j in range(group):
+                    unless_own(c, j, lambda s: near_copy(q, s).wait_recv())
 
         def gathered(low):
             return jnp.concatenate(
@@ -236,18 +323,35 @@
                 parts[q - 1, span, :, low : low + width] = part.reshape(
                     group, capacity, width
                 ).astype(jnp.bfloat16)
-        for q in range(1, replicas):
-            part_copy(q, c).start()
+
+        @pl.when(c >= near_chunks)
+        def _():
+            for q in range(1, replicas):
+                part_copy(q, c).start()
+
+        @pl.when(c < near_chunks)
+        def _():
+            for q in range(1, replicas):
+                for j in range(group):
+                    unless_own(c, j, lambda s: return_copy(q, s).start())
 
     def give_back(c):
         span = pl.ds(c * group, group)
         place_rows = pl.ds(pl.multiple_of(c * chunk_rows, chunk_rows), chunk_rows)
-        for q in range(1, replicas):
-            part_copy(q, c).wait_recv()
         total = own[place_rows, :].reshape(group, capacity, 2 * width)
-        for q in range(1, replicas):
-            total = total + part_recv[q - 1, span].astype(jnp.float32)
-        outgoing[span] = total.astype(jnp.bfloat16)
+
+        @pl.when(c < near_chunks)
+        def _():
+            outgoing[span] = total.astype(jnp.bfloat16)
+
+        @pl.when(c >= near_chunks)
+        def _():
+            whole = total
+            for q in range(1, replicas):
+                part_copy(q, c).wait_recv()
+                whole = whole + part_recv[q - 1, span].astype(jnp.float32)
+            outgoing[span] = whole.astype(jnp.bfloat16)
+
         for j in range(group):
             unless_own(c, j, lambda s: back_copy(s).start())
 
@@ -266,6 +370,20 @@
             give_back(turn(t - 2))
 
     back[0] = outgoing[0]
+
+    for q in range(1, replicas):
+        near_back[q - 1, 0] = parts[q - 1, 0]
+
+        @pl.loop(1, near)
+        def _(s):
+            return_copy(q, s).wait_recv()
+
+        for chosen, low in ((other_gate, 0), (other_pick, width)):
+            values = near_back[q - 1, :, :, low : low + width].reshape(near * capacity, width)
+            sums_out[q - 1, :, low : low + width] = product(chosen[q - 1], values, 1, 0).astype(
+                jnp.bfloat16
+            )
+        sums_copy(q).start()
 
     for low in range(0, hidden, hidden_tile):
         high = low + hidden_tile
@@ -280,11 +398,19 @@
     def _(s):
         back_copy(s).wait_recv()
 
-    returned = back[:, :, :width].reshape(slot_count, width)
-    moe_output[...] = product(slot_gate[...], returned, 1, 0).astype(jnp.bfloat16)
+    for q in range(1, replicas):
+        sums_copy(q).wait_recv()
+
+    def combined(chosen, low):
+        returned = back[:, :, low : low + width].reshape(slot_count, width)
+        total = product(chosen[...], returned, 1, 0)
+        for q in range(1, replicas):
+            total = total + sums_in[q - 1, :, low : low + width].astype(jnp.float32)
+        return total
+
+    moe_output[...] = combined(slot_gate, 0).astype(jnp.bfloat16)
     x_float, inv_rms, gain_rows = norm_parts()
-    returned = back[:, :, width:].reshape(slot_count, width)
-    scaled = gain_rows * product(slot_pick[...], returned, 1, 0)
+    scaled = gain_rows * combined(slot_pick, width)
     inner = jnp.mean(x_float * scaled, axis=-1, keepdims=True)
     token_grad[...] = (
         inv_rms * scaled - x_float * (inv_rms * inv_rms * inv_rms) * inner
@@ -295,9 +421,18 @@
         in_copy(s).wait_send()
         back_copy(s).wait_send()
 
-    @pl.loop(0, chunks)
-    def _(c):
-        for q in range(1, replicas):
+    for q in range(1, replicas):
+        marks_copy(q).wait_send()
+        dense_copy(q).wait_send()
+        sums_copy(q).wait_send()
+
+        @pl.loop(1, near)
+        def _(s):
+            near_copy(q, s).wait_send()
+            return_copy(q, s).wait_send()
+
+        @pl.loop(near_chunks, chunks)
+        def _(c):
             fwd_copy(q, c).wait_send()
             part_copy(q, c).wait_send()
 
@@ -344,6 +479,21 @@
             dma((replicas - 1, chunks)),
             dma((experts,)),
             dma((experts,)),
+            pltpu.VMEM((8, tok_count), jnp.int32),
+            pltpu.VMEM((replicas - 1, 8, tok_count), jnp.int32),
+            pltpu.VMEM((tok_count, 2 * width), half),
+            pltpu.VMEM((replicas - 1, tok_count, 2 * width), half),
+            pltpu.VMEM((replicas - 1, experts // 2, capacity, 2 * width), half),
+            pltpu.VMEM((replicas - 1, experts // 2, capacity, 2 * width), half),
+            pltpu.VMEM((replicas - 1, tok_count, 2 * width), half),
+            pltpu.VMEM((replicas - 1, tok_count, 2 * width), half),
+            pltpu.VMEM((replicas - 1, tok_count, slots // 2), half),
+            pltpu.VMEM((replicas - 1, tok_count, slots // 2), half),
+            dma((2, replicas - 1)),
+            dma((2, replicas - 1)),
+            dma((2, replicas - 1)),
+            dma((2, replicas - 1, experts // 2)),
+            dma((2, replicas - 1, experts // 2)),
         ],
         compiler_params=pltpu.CompilerParams(
             collective_id=0, has_side_effects=True, vmem_limit_bytes=56 * 1024 * 1024

time: 74.3 us -> 67.5 us (0.908)
  Pallas kernels: 67.7 us -> 61 us
    pallas_call x1, Pallas kernels: 67.7 us -> 61 us  [on_device(): pl.pallas_call(functools.partial(layer_kernel, experts, replicas, chunks)...]
where the time goes in v4:
time: 67.5 us; the launch traced here: 67.3 us
  Pallas kernels  61 us (90%)
  local copies, waits for them, and re-layouts  5.59 us (8%)
    pallas_call x1, Pallas kernels, on_device(): pl.pallas_call(functools.partial(layer_kernel, experts, replicas, chunks)...  61 us
    unnamed x8, local copies, waits for them, and re-layouts  5.59 us

profile of v4, /device:TPU:0, one launch (start us, length us, event | category | flops | bytes accessed | tf_op | source)
XLA Modules:
  0.0 67.3 jit_solution(986367238026853400)
XLA Ops:
  0.6 61.0 %shard_map.111 = (bf16[128,512]{1,0:T(8,128)(2,1)}, bf16[128,512]{1,0:T(8,128)(2,1)}, bf16[1024,512]{1,0:T(8,128)(2,1)}, bf16[1024,512]{1,0:T(8,128)(2,1)}) custom-call(bf16[128,512]{1,0:T(8,128)(2,1)} %tokens.1, s32[1,128]{1,0:T(1,128)} %bitcast.12, f32[2,512]{1,0:T(2,128)} %gains.1, s32[2,128]{1,0:T(2,128)} %bitcast.11, s32[1,128]{1,0:T(1,128)} %bitcast.13, ...), custom_call_target="tpu_custom_call" | custom-call | tf_op jit(solution)/shard_map/pallas_call | solution.py:452
  61.7 0.0 copy-start.1
  61.7 1.6 %copy.16 = bf16[128,512]{1,0:T(8,128)(2,1)} copy(bf16[128,512]{1,0:T(8,128)(2,1)} %get-tuple-element.16) | data formatting | bytes 262144
  63.3 0.0 copy-done.1
  63.3 0.7 copy.17
  63.9 0.0 copy-start
  63.9 2.4 %copy.18 = bf16[1,1024,512]{2,1,0:T(8,128)(2,1)} copy(bf16[1,1024,512]{2,1,0:T(8,128)(2,1)} %bitcast.8) | data formatting | bytes 2097152
  66.3 0.0 copy-done
  66.3 1.0 %copy.19 = bf16[1,1024,512]{2,1,0:T(8,128)(2,1)} copy(bf16[1,1024,512]{2,1,0:T(8,128)(2,1)S(1)} %bitcast.7) | data formatting | bytes 2097152
Async XLA Ops:
  61.7 1.6 %copy-start.1 = (bf16[128,512]{1,0:T(8,128)(2,1)S(1)}, bf16[128,512]{1,0:T(8,128)(2,1)}, u32[]{:S(2)}) copy-start(bf16[128,512]{1,0:T(8,128)(2,1)} %get-tuple-element.17) | copy-start | bytes 393220
  63.9 2.4 %copy-start = (bf16[1024,512]{1,0:T(8,128)(2,1)S(1)}, bf16[1024,512]{1,0:T(8,128)(2,1)}, u32[]{:S(2)}) copy-start(bf16[1024,512]{1,0:T(8,128)(2,1)} %get-tuple-element.11) | copy-start | bytes 3145732

commit v5 on v4

--- a/solution.py
+++ b/solution.py
@@ -27,13 +27,13 @@
     gains,
     routes,
     gate_share,
-    up,
-    down,
+    up_home,
+    down_home,
     cotangent,
     moe_output,
     token_grad,
-    up_grad,
-    down_grad,
+    up_out,
+    down_out,
     send,
     recv,
     parts,
@@ -68,6 +68,11 @@
     sums_sems,
     near_sems,
     return_sems,
+    up,
+    down,
+    up_grad,
+    down_grad,
+    local_sems,
 ):
     me = lax.axis_index("expert")
     dp = lax.axis_index("dp")
@@ -182,6 +187,13 @@
             device_id={"dp": (dp + replicas - q) % replicas},
             device_id_type=MESH,
         )
+
+    up_load = pltpu.make_async_copy(up_home, up, local_sems.at[0])
+    down_load = pltpu.make_async_copy(down_home, down, local_sems.at[1])
+    up_store = pltpu.make_async_copy(up_grad, up_out, local_sems.at[2])
+    down_store = pltpu.make_async_copy(down_grad, down_out, local_sems.at[3])
+    up_load.start()
+    down_load.start()
 
     barrier = pltpu.get_barrier_semaphore()
 
@@ -355,6 +367,9 @@
         for j in range(group):
             unless_own(c, j, lambda s: back_copy(s).start())
 
+    up_load.wait()
+    down_load.wait()
+
     @pl.loop(0, chunks + 2)
     def _(t):
         @pl.when(t < chunks)
@@ -394,6 +409,9 @@
                 total = total + product(store[q, :, low:high], rows, 0, 0)
             target[low:high, :] = (total * grad_scale).astype(jnp.bfloat16)
 
+    up_store.start()
+    down_store.start()
+
     @pl.loop(1, experts)
     def _(s):
         back_copy(s).wait_recv()
@@ -415,6 +433,9 @@
     token_grad[...] = (
         inv_rms * scaled - x_float * (inv_rms * inv_rms * inv_rms) * inner
     ).astype(jnp.bfloat16)
+
+    up_store.wait()
+    down_store.wait()
 
     @pl.loop(1, experts)
     def _(s):
@@ -449,6 +470,7 @@
     blocks = (experts, capacity, 2 * width)
     dma = pltpu.SemaphoreType.DMA
     in_vmem = pl.BlockSpec(memory_space=pltpu.VMEM)
+    anywhere = pl.BlockSpec(memory_space=pl.ANY)
     moe_output, token_grad, up_grad, down_grad = pl.pallas_call(
         functools.partial(layer_kernel, experts, replicas, chunks),
         out_shape=(
@@ -457,8 +479,8 @@
             jax.ShapeDtypeStruct((hidden, width), half),
             jax.ShapeDtypeStruct((hidden, width), half),
         ),
-        in_specs=[in_vmem] * 8,
-        out_specs=(in_vmem,) * 4,
+        in_specs=[in_vmem] * 5 + [anywhere] * 2 + [in_vmem],
+        out_specs=(in_vmem, in_vmem, anywhere, anywhere),
         scratch_shapes=[
             pltpu.VMEM(blocks, half),
             pltpu.VMEM((replicas,) + blocks, half),
@@ -494,9 +516,14 @@
             dma((2, replicas - 1)),
             dma((2, replicas - 1, experts // 2)),
             dma((2, replicas - 1, experts // 2)),
+            pltpu.VMEM((hidden, width), half),
+            pltpu.VMEM((hidden, width), half),
+            pltpu.VMEM((hidden, width), half),
+            pltpu.VMEM((hidden, width), half),
+            dma((4,)),
         ],
         compiler_params=pltpu.CompilerParams(
-            collective_id=0, has_side_effects=True, vmem_limit_bytes=56 * 1024 * 1024
+            collective_id=0, has_side_effects=True, vmem_limit_bytes=min(56, 12 + 10 * replicas) * 1024 * 1024
         ),
     )(
         tokens,

time: 67.5 us -> 66.7 us (0.988)
  Pallas kernels: 61 us -> 57.5 us
  local copies, waits for them, and re-layouts: 5.59 us -> 8.19 us
    pallas_call x1, Pallas kernels: 61 us -> 57.5 us  [on_device(): pl.pallas_call(functools.partial(layer_kernel, experts, replicas, chunks)...]
    unnamed x8 -> x20, local copies, waits for them, and re-layouts: 5.59 us -> 8.19 us
where the time goes in v5:
time: 66.7 us; the launch traced here: 66.4 us
  Pallas kernels  57.5 us (86%)
  local copies, waits for them, and re-layouts  8.19 us (12%)
  between operations  0.68 us (1%)
    pallas_call x1, Pallas kernels, on_device(): pl.pallas_call(functools.partial(layer_kernel, experts, replicas, chunks)...  57.5 us
    unnamed x20, local copies, waits for them, and re-layouts  8.19 us

profile of v5, /device:TPU:0, one launch (start us, length us, event | category | flops | bytes accessed | tf_op | source)
XLA Modules:
  0.0 66.4 jit_solution(9490661976026947196)
XLA Ops:
  0.6 0.0 copy-start.4
  0.6 0.0 copy-start.7
  0.7 0.0 copy-start.5
  0.7 0.0 copy-start.6
  0.7 0.6 copy-done.4
  1.3 0.0 copy-done.7
  1.3 0.0 copy-done.5
  1.3 0.0 copy-done.6
  1.3 0.0 copy-start
  1.4 1.2 %copy-done = bf16[1,1024,512]{2,1,0:T(8,128)(2,1)S(1)} copy-done((bf16[1,1024,512]{2,1,0:T(8,128)(2,1)S(1)}, bf16[1,1024,512]{2,1,0:T(8,128)(2,1)}, u32[]{:S(2)}) %copy-start) | copy-done | bytes 1048600
  2.6 0.0 copy-start.1
  2.6 1.2 %copy-done.1 = bf16[1,1024,512]{2,1,0:T(8,128)(2,1)S(1)} copy-done((bf16[1,1024,512]{2,1,0:T(8,128)(2,1)S(1)}, bf16[1,1024,512]{2,1,0:T(8,128)(2,1)}, u32[]{:S(2)}) %copy-start.1) | copy-done | bytes 1048600
  3.8 0.0 copy-start.2
  3.8 0.9 %copy-done.2 = bf16[128,512]{1,0:T(8,128)(2,1)S(1)} copy-done((bf16[128,512]{1,0:T(8,128)(2,1)S(1)}, bf16[128,512]{1,0:T(8,128)(2,1)}, u32[]{:S(2)}) %copy-start.2) | copy-done | bytes 131096
  4.7 0.0 copy-start.3
  4.7 0.9 %copy-done.3 = bf16[128,512]{1,0:T(8,128)(2,1)S(1)} copy-done((bf16[128,512]{1,0:T(8,128)(2,1)S(1)}, bf16[128,512]{1,0:T(8,128)(2,1)}, u32[]{:S(2)}) %copy-start.3) | copy-done | bytes 131096
  5.6 57.5 %shard_map.111 = (bf16[128,512]{1,0:T(8,128)(2,1)S(1)}, bf16[128,512]{1,0:T(8,128)(2,1)S(1)}, bf16[1024,512]{1,0:T(8,128)(2,1)S(1)}, bf16[1024,512]{1,0:T(8,128)(2,1)S(1)}) custom-call(bf16[128,512]{1,0:T(8,128)(2,1)S(1)} %copy-done.2, s32[1,128]{1,0:T(1,128)S(1)} %bitcast.12, f32[2,512]{1,0:T(2,128)S(1)} %copy-done.4, s32[2,128]{1,0:T(2,128)S(1)} %bitcast.11, ...), custom_call_target="tpu_custom_call" | custom-call | tf_op jit(solution)/shard_map/pallas_call | solution.py:474
  63.2 0.7 copy.16
  63.8 0.7 copy.17
  64.5 1.0 %copy.18 = bf16[1,1024,512]{2,1,0:T(8,128)(2,1)} copy(bf16[1,1024,512]{2,1,0:T(8,128)(2,1)S(1)} %bitcast.8) | data formatting | bytes 2097152
  65.4 1.0 %copy.19 = bf16[1,1024,512]{2,1,0:T(8,128)(2,1)} copy(bf16[1,1024,512]{2,1,0:T(8,128)(2,1)S(1)} %bitcast.7) | data formatting | bytes 2097152
Async XLA Ops:
  0.6 0.7 %copy-start.4 = (f32[2,512]{1,0:T(2,128)S(1)}, f32[2,512]{1,0:T(2,128)}, u32[]{:S(2)}) copy-start(f32[2,512]{1,0:T(2,128)} %gains.1) | copy-start | bytes 12292
  0.6 0.7 %copy-start.7 = (s32[128]{0:T(128)S(1)}, s32[128]{0:T(128)}, u32[]{:S(2)}) copy-start(s32[128]{0:T(128)} %param.12) | copy-start | bytes 1540
  0.7 0.7 %copy-start.5 = (s32[128,2]{0,1:T(2,128)S(1)}, s32[128,2]{0,1:T(2,128)}, u32[]{:S(2)}) copy-start(s32[128,2]{0,1:T(2,128)} %param.11) | copy-start | bytes 3076
  0.7 0.7 %copy-start.6 = (s32[128]{0:T(128)S(1)}, s32[128]{0:T(128)}, u32[]{:S(2)}) copy-start(s32[128]{0:T(128)} %param.9) | copy-start | bytes 1540
  1.3 1.2 %copy-start = (bf16[1,1024,512]{2,1,0:T(8,128)(2,1)S(1)}, bf16[1,1024,512]{2,1,0:T(8,128)(2,1)}, u32[]{:S(2)}) copy-start(bf16[1,1024,512]{2,1,0:T(8,128)(2,1)} %param.13) | copy-start | bytes 3145732
  2.6 1.2 %copy-start.1 = (bf16[1,1024,512]{2,1,0:T(8,128)(2,1)S(1)}, bf16[1,1024,512]{2,1,0:T(8,128)(2,1)}, u32[]{:S(2)}) copy-start(bf16[1,1024,512]{2,1,0:T(8,128)(2,1)} %param.14) | copy-start | bytes 3145732
  3.8 0.9 %copy-start.2 = (bf16[128,512]{1,0:T(8,128)(2,1)S(1)}, bf16[128,512]{1,0:T(8,128)(2,1)}, u32[]{:S(2)}) copy-start(bf16[128,512]{1,0:T(8,128)(2,1)} %tokens.1) | copy-start | bytes 393220
  4.7 0.9 %copy-start.3 = (bf16[128,512]{1,0:T(8,128)(2,1)S(1)}, bf16[128,512]{1,0:T(8,128)(2,1)}, u32[]{:S(2)}) copy-start(bf16[128,512]{1,0:T(8,128)(2,1)} %cotangent.1) | copy-start | bytes 393220
